TPU v7x, 512 devices: a whole 4x4x16 slice. The times are simulated.
512 devices in a mesh: expert: 64 (over y, x, z_hi, core), mp: 8 (over z_lo).
Axes of the slice: x: 4, y: 4, z: 16 (z_hi: 2, z_lo: 8; z = z_hi * 8 + z_lo), core: 2. Of those that a mesh axis runs over, the one named last changes fastest.
Arguments:
- tokens: bfloat16 [8192, 3584], P('expert'), may hold values from -6 to 6
- routes: int32 [8192, 2], P('expert'), may hold values from 0 to 31, all different within a row; in each aligned block of 128 rows (0 to 127, 128 to 255, ...) at most 16 rows name the same one
- gate_values: float32 [8192, 2], P('expert'), may hold values from 0.2 to 1
- expert_weights: bfloat16 [64, 3, 1792, 1024], P('expert', None, None, 'mp'), may hold values from -0.09375 to 0.09375
- old_owner: int32 [32], replicated, may hold values from 0 to 31, as said below
- new_owner: int32 [32], replicated, may hold values from 0 to 31, as said below
Outputs:
- mixed: bfloat16 [8192, 3584], P('expert', 'mp')
- relocated: bfloat16 [64, 3, 1792, 1024], P('expert', None, None, 'mp')
Inputs may be any that keep to these rules, and one draw needn't show every extreme that they name: `routes`: in each aligned block of 128 rows (the rows of one index of expert) no expert is named by more than 16 rows. `old_owner`: each slot holds exactly one expert. Each slot holds exactly one expert; exactly 2 experts have a new_owner other than their old_owner.
All inputs are finite; a program needn't handle non-finite values.
Results may differ from a plain program's by a relative error of at most 0.019.
Values may be sent and summed in bfloat16 or wider, within the bound.
No kernel may reach another device: no remote copies, remote signals or barrier semaphores. Data moves between devices by JAX's collectives and lax.ppermute only.
A program may use at most 64 MiB of HBM per device.

v0:
```python
import jax
import jax.numpy as jnp
from jax import lax
from jax.experimental.layout import Layout, with_layout_constraint
from jax.sharding import Mesh, PartitionSpec as P

PLANE = ("y", "x", "c")
NEAR = ("mb", "mc")
RING = ("zh", "ma", "mb", "mc")
CAP = 16


def swap(value, axis):
    return lax.ppermute(value, axis, [(0, 1), (1, 0)])


def mirrored(value):
    return lax.ppermute(value, RING, [(i, 15 - i) for i in range(16)])


def place_codes(routes, gate_values, owner):
    experts = owner.shape[0]
    flat = routes.T.reshape(-1)
    count = flat.shape[0]
    ids = jnp.arange(experts, dtype=jnp.int32)
    hot = (flat[:, None] == ids[None, :]).astype(jnp.bfloat16)
    at = jnp.arange(count, dtype=jnp.int32)
    earlier = (at[:, None] > at[None, :]).astype(jnp.bfloat16)
    before = jnp.dot(earlier, hot, preferred_element_type=jnp.float32)
    code = jnp.sum(
        hot.astype(jnp.float32) * (before + (owner * CAP).astype(jnp.float32)[None, :]), axis=1
    )
    return jnp.concatenate([code.reshape(routes.shape[1], -1), gate_values.T], axis=0)


def placed_rows(codes, zh):
    code = codes[:2].astype(jnp.int32)
    slot, rank = (code // CAP, code % CAP)
    row = jnp.where(slot % 2 == zh, slot // 2 * (2 * CAP) + rank, -2 * CAP)
    return jnp.stack([row, row + CAP], axis=1).reshape(2, -1)


def plane_rows():
    return 2 * CAP * lax.axis_size("y") * lax.axis_size("x")


def gather_rows(rows, table):
    at = jnp.arange(plane_rows(), dtype=jnp.int32)
    pick = ((rows[0][None, :] == at[:, None]) | (rows[1][None, :] == at[:, None])).astype(
        jnp.bfloat16
    )
    return jnp.dot(pick, table, preferred_element_type=jnp.float32).astype(jnp.bfloat16)


def exchange(rows, axes=PLANE):
    blocks = rows.reshape((lax.axis_size(axes), -1, rows.shape[-1]))
    return lax.all_to_all(blocks, axes, split_axis=0, concat_axis=0, tiled=True).reshape(rows.shape)


def expert_part(rows, weights):
    half = jnp.einsum("rd,gdf->grf", rows, weights[:2], preferred_element_type=jnp.float32)
    total = half + swap(half, "c")
    hidden = (jax.nn.silu(total[0]) * total[1]).astype(jnp.bfloat16)
    return lax.dot_general(
        hidden, weights[2], (((1,), (1,)), ((), ())), preferred_element_type=jnp.float32
    ).astype(jnp.bfloat16)


def weighted(back, codes, rows):
    at = jnp.arange(back.shape[0], dtype=jnp.int32)
    gate = jnp.concatenate([codes[2:4], codes[2:4]], axis=1)
    mix = sum((jnp.where(rows[k][:, None] == at[None, :], gate[k][:, None], 0.0) for k in range(2)))
    high = mix.astype(jnp.bfloat16)
    low = (mix - high.astype(jnp.float32)).astype(jnp.bfloat16)
    return jnp.dot(high, back, preferred_element_type=jnp.float32) + jnp.dot(
        low, back, preferred_element_type=jnp.float32
    )


def by_columns(mixed, near):
    tok_rows = mixed.shape[0] // 2
    parts = mixed.astype(jnp.bfloat16).reshape(2, tok_rows, 2, near, -1)
    return jnp.transpose(parts, (3, 2, 1, 0, 4)).reshape(near, 2, tok_rows, -1)


def near_sum(parts, place, mine, beside):
    count = parts.shape[0]
    own = lax.dynamic_index_in_dim(parts, place ^ mine, 0, keepdims=False)
    own, beside = tied((own, beside))
    total = own.astype(jnp.float32)
    for step in range(1, count):
        block = lax.dynamic_index_in_dim(parts, place ^ step ^ mine, 0, keepdims=False)
        total += lax.ppermute(block, NEAR, [(i, i ^ step) for i in range(count)]).astype(
            jnp.float32
        )
    return (total.astype(jnp.bfloat16), beside)


tied = lax.optimization_barrier


def pick_pieces(spread, old_owner, new_owner, zh):
    moved = new_owner != old_owner
    low = jnp.min(jnp.where(moved, old_owner, old_owner.shape[0]))
    high = jnp.max(jnp.where(moved, old_owner, -1))
    low_piece = lax.dynamic_index_in_dim(spread, low >> 1, 0, keepdims=False)
    high_piece = lax.dynamic_index_in_dim(spread, high >> 1, 0, keepdims=False)
    low_here, high_here = (low & 1 == zh, high & 1 == zh)
    other = swap(jnp.where(low_here, low_piece, high_piece), "zh")
    to_low = jnp.where(high_here, high_piece, other)
    to_high = jnp.where(low_here, low_piece, other)
    slots = 2 * jnp.arange(spread.shape[0], dtype=jnp.int32)[:, None, None] + zh
    return jnp.where(slots == low, to_low[None], jnp.where(slots == high, to_high[None], spread))


def shards(tokens, routes, gate_values, expert_weights, old_owner, new_owner):
    zh, far, place = (lax.axis_index("zh"), lax.axis_index("ma"), lax.axis_index(NEAR))
    near = lax.axis_size(NEAR)
    tok_rows = tokens.shape[0]
    own = expert_weights[0]
    table = jnp.transpose(tokens.reshape(tok_rows, 2 * near, 2, -1), (2, 0, 1, 3)).reshape(
        2 * tok_rows, -1
    )
    table = with_layout_constraint(table, Layout(major_to_minor=(0, 1)))
    share = 2 * tok_rows // near
    part = lax.dynamic_slice_in_dim(table, (near - 1 - place) * share, share, 0)
    codes = place_codes(routes, gate_values, old_owner)
    rows = placed_rows(codes, zh)
    quarter = mirrored(part)
    chips = lax.axis_size("y") * lax.axis_size("x")
    spread = lax.all_to_all(
        own.reshape(chips, -1, own.shape[-1]), ("y", "x"), split_axis=0, concat_axis=0, tiled=True
    )
    other_codes = mirrored(codes)
    payload, spread, quarter, other_codes = tied(
        (gather_rows(rows, table), spread, quarter, other_codes)
    )
    sent = exchange(payload)
    other_rows = placed_rows(other_codes, zh)
    other_table = lax.all_gather(quarter, NEAR, tiled=True)
    payload, sent = tied((gather_rows(other_rows, other_table), sent))
    other_sent = exchange(payload)
    chosen = pick_pieces(spread, old_owner, new_owner, zh)
    payload, other_sent, chosen = tied((expert_part(sent, own), other_sent, chosen))
    back = exchange(payload)
    payload, back = tied((expert_part(other_sent, own), back))
    other_back = exchange(payload)
    parts = by_columns(weighted(back, codes, rows), near)
    kept, other_back = near_sum(parts, place, 0, other_back)
    other_parts = by_columns(weighted(other_back, other_codes, other_rows), near)
    other_kept, chosen = near_sum(other_parts, place, near - 1, chosen)
    arrived = lax.all_to_all(chosen, ("y", "x"), split_axis=0, concat_axis=0, tiled=True)

    def of(value, index):
        return lax.dynamic_index_in_dim(value, index, 0, keepdims=False)

    total = of(kept, far).astype(jnp.float32)
    total += swap(of(kept, 1 - far), "ma").astype(jnp.float32)
    total += mirrored(of(other_kept, 1 - far)).astype(jnp.float32)
    total += lax.ppermute(of(other_kept, far), RING, [(i, i ^ 11) for i in range(16)]).astype(
        jnp.float32
    )
    return (total.astype(jnp.bfloat16), arrived.reshape(expert_weights.shape))


def solution(mesh):
    fine = Mesh(mesh.devices.reshape(4, 4, 2, 2, 2, 2, 2), ("y", "x", "zh", "c", "ma", "mb", "mc"))
    expert, mp = (("y", "x", "zh", "c"), ("ma", "mb", "mc"))
    in_specs = (
        P(expert, None),
        P(expert, None),
        P(expert, None),
        P(expert, None, None, mp),
        P(),
        P(),
    )
    out_specs = (P(expert, mp), P(expert, None, None, mp))
    return jax.shard_map(shards, mesh=fine, in_specs=in_specs, out_specs=out_specs, check_vma=False)
```

profile of v0, /device:TPU:99, one launch (start us, length us, event | category | flops | bytes accessed | tf_op | source)
XLA Modules:
  0.0 237.3 jit_solution(9027821609001539932)
XLA Ops:
  0.6 7.1 %all-to-all-start = ((bf16[16,336,128]{2,1,0:T(8,128)(2,1)}), bf16[16,336,128]{2,1,0:T(8,128)(2,1)S(1)}, u32[]{:S(2)}, u32[]{:S(2)}) async-start(bf16[16,336,128]{2,1,0:T(8,128)(2,1)} %bitcast.112), calls=%async_computation | async-start | bytes 2752512 | tf_op jit(solution)/shard_map/all_to_all | solution.py:131
  7.7 0.6 copy.9
  8.4 0.9 copy.16
  9.3 1.3 reshape.274
  10.6 11.1 %collective-permute-start = (bf16[64,1792]{1,0:T(8,128)(2,1)S(1)}, bf16[64,1792]{1,0:T(8,128)(2,1)S(1)}, u32[]{:S(2)}, u32[]{:S(2)}) collective-permute-start(bf16[64,1792]{1,0:T(8,128)(2,1)S(1)} %constant_dynamic-slice_fusion), channel_id=1, source_target_pairs={{0,23},{1,22},{2,21},{3,20},{4,19},{5,18},{6,17},{7,16},{16,7},{17... | collective-permute-start | bytes 688136 | tf_op jit(solution)/shard_map/ppermute | solution.py:18
  21.7 0.6 fusion.67
  22.4 0.2 fusion.13
  22.6 1.9 collective-permute-start.1
  24.6 1.9 convolution_convert_fusion.1
  26.5 7.1 %collective-permute-done.1 = f32[4,128]{1,0:T(4,128)S(1)} collective-permute-done((f32[4,128]{1,0:T(4,128)S(1)}, f32[4,128]{1,0:T(4,128)S(1)}, u32[]{:S(2)}, u32[]{:S(2)}) %collective-permute-start.1) | collective-permute-done | bytes 2080 | tf_op jit(solution)/shard_map/ppermute | solution.py:18
  33.6 9.8 %all-to-all-start.1 = ((bf16[32,16,1792]{2,1,0:T(8,128)(2,1)}), bf16[32,16,1792]{2,1,0:T(8,128)(2,1)S(1)}, u32[]{:S(2)}, u32[]{:S(2)}) async-start(bf16[32,16,1792]{2,1,0:T(8,128)(2,1)} %bitcast.16), calls=%async_computation.1 | async-start | bytes 3670016 | tf_op jit(solution)/shard_map/all_to_all | solution.py:57
  43.4 21.5 %all_gather.3 = bf16[256,1792]{1,0:T(8,128)(2,1)S(1)} all-gather(bf16[64,1792]{1,0:T(8,128)(2,1)S(1)} %collective-permute-done), channel_id=1, replica_groups=mesh['y'=4,'x'=4,'zh'=2,'c'=2,'ma'=2,'mb'=2,'mc'=2] {'mb','mc'}, dimensions={0}, use_global_device_ids=true | all-gather | bytes 1146880 | tf_op jit(solution)/shard_map/all_gather | solution.py:140
  65.0 1.9 convolution_convert_fusion
  66.9 0.9 all-to-all-done.1
  67.7 1.3 copy-done.3
  69.0 8.6 %all-to-all-start.2 = ((bf16[32,16,1792]{2,1,0:T(8,128)(2,1)}), bf16[32,16,1792]{2,1,0:T(8,128)(2,1)}, u32[]{:S(2)}, u32[]{:S(2)}) async-start(bf16[32,16,1792]{2,1,0:T(8,128)(2,1)} %bitcast.23), calls=%async_computation.2 | async-start | bytes 3670016 | tf_op jit(solution)/shard_map/all_to_all | solution.py:57
  80.2 1.3 fusion.69
  81.5 8.9 %collective-permute-start.3 = (bf16[336,128]{1,0:T(8,128)(2,1)S(1)}, bf16[336,128]{1,0:T(8,128)(2,1)S(1)}, u32[]{:S(2)}, u32[]{:S(2)}) collective-permute-start(bf16[336,128]{1,0:T(8,128)(2,1)S(1)} %bitcast_select_fusion.1), channel_id=1, source_target_pairs={{0,16},{16,0},{1,17},{17,1},{2,18},{18,2},{3,19},{19,3},{4,20},{20... | collective-permute-start | bytes 258056 | tf_op jit(solution)/shard_map/ppermute | solution.py:14
  90.4 2.1 fusion.6
  92.6 2.5 %collective-permute-start.2 = (f32[2,512,128]{2,1,0:T(8,128)S(1)}, f32[2,512,128]{2,1,0:T(8,128)S(1)}, u32[]{:S(2)}, u32[]{:S(2)}) collective-permute-start(f32[2,512,128]{2,1,0:T(8,128)S(1)} %fusion.6), channel_id=1, source_target_pairs={{0,8},{8,0},{1,9},{9,1},{2,10},{10,2},{3,11},{11,3},{4,12},{12,4},... | collective-permute-start | bytes 1572872 | tf_op jit(solution)/shard_map/ppermute | solution.py:14
  95.1 0.7 collective-permute-done.3
  95.9 1.3 select_select_fusion
  97.2 0.1 add.231
  97.3 1.9 convolution_convert_fusion.3
  99.2 2.8 %all-to-all-done.2 = bf16[32,16,1792]{2,1,0:T(8,128)(2,1)} async-done(((bf16[32,16,1792]{2,1,0:T(8,128)(2,1)}), bf16[32,16,1792]{2,1,0:T(8,128)(2,1)}, u32[]{:S(2)}, u32[]{:S(2)}) %all-to-all-start.2) | async-done | bytes 1835040 | tf_op jit(solution)/shard_map/all_to_all | solution.py:57
  102.0 7.5 %all-to-all-start.3 = ((bf16[32,16,1792]{2,1,0:T(8,128)(2,1)}), bf16[32,16,1792]{2,1,0:T(8,128)(2,1)S(1)}, u32[]{:S(2)}, u32[]{:S(2)}) async-start(bf16[32,16,1792]{2,1,0:T(8,128)(2,1)} %bitcast.110), calls=%async_computation.3 | async-start | bytes 3670016 | tf_op jit(solution)/shard_map/all_to_all | solution.py:57
  109.4 2.1 fusion.9
  111.6 2.3 collective-permute-start.4
  113.9 1.5 collective-permute-done.4
  115.4 0.1 add.237
  115.5 1.9 convolution_convert_fusion.2
  117.4 16.4 %all-to-all-done.3 = bf16[32,16,1792]{2,1,0:T(8,128)(2,1)S(1)} async-done(((bf16[32,16,1792]{2,1,0:T(8,128)(2,1)}), bf16[32,16,1792]{2,1,0:T(8,128)(2,1)S(1)}, u32[]{:S(2)}, u32[]{:S(2)}) %all-to-all-start.3) | async-done | bytes 1835040 | tf_op jit(solution)/shard_map/all_to_all | solution.py:57
  133.8 1.2 copy-done
  135.0 6.5 %all-to-all-start.4 = ((bf16[32,16,1792]{2,1,0:T(8,128)(2,1)}), bf16[32,16,1792]{2,1,0:T(8,128)(2,1)S(1)}, u32[]{:S(2)}, u32[]{:S(2)}) async-start(bf16[32,16,1792]{2,1,0:T(8,128)(2,1)} %bitcast.109), calls=%async_computation.4 | async-start | bytes 3670016 | tf_op jit(solution)/shard_map/all_to_all | solution.py:57
  141.6 2.4 fusion.45
  144.0 1.7 fusion
  145.7 3.5 %reshape.275 = bf16[2,128,2,4,224]{4,3,2,1,0:T(4,128)(2,1)S(1)} reshape(bf16[256,1792]{1,0:T(8,128)(2,1)} %fusion) | data formatting | bytes 1835008 | tf_op jit(solution)/shard_map/reshape | solution.py:82
  149.2 2.3 copy.18
  151.5 1.3 copy.13
  152.8 0.8 dynamic-slice_bitcast_fusion.6
  153.5 1.9 collective-permute-start.5
  155.5 10.1 %collective-permute-start.6 = (bf16[2,128,448]{1,2,0:T(8,128)(2,1)S(1)}, bf16[2,128,448]{1,2,0:T(8,128)(2,1)}, u32[]{:S(2)}, u32[]{:S(2)}) collective-permute-start(bf16[2,128,448]{1,2,0:T(8,128)(2,1)S(1)} %get-tuple-element.42), channel_id=1, source_target_pairs={{0,2},{1,3},{2,0},{3,1},{4,6},{5,7},{6,4},{7,5},{8,10},{9,11},{10,... | collective-permute-start | bytes 688136 | tf_op jit(solution)/shard_map/ppermute | solution.py:93
  165.5 1.9 collective-permute-start.7
  167.5 0.7 fusion.48
  168.2 0.8 fusion.1
  169.0 1.5 reshape.276
  170.5 1.4 copy.19
  171.9 0.1 copy.15
  172.0 0.1 dynamic-slice_bitcast_fusion.3
  172.1 6.8 %all-to-all-start.5 = ((bf16[16,336,128]{2,1,0:T(8,128)(2,1)}), bf16[16,336,128]{2,1,0:T(8,128)(2,1)S(1)}, u32[]{:S(2)}, u32[]{:S(2)}) async-start(bf16[16,336,128]{2,1,0:T(8,128)(2,1)} %select_select_fusion), calls=%async_computation.5 | async-start | bytes 2752512 | tf_op jit(solution)/shard_map/all_to_all | solution.py:152
  178.9 3.1 %collective-permute-start.10 = (bf16[2,128,448]{1,2,0:T(8,128)(2,1)S(1)}, bf16[2,128,448]{1,2,0:T(8,128)(2,1)S(1)}, u32[]{:S(2)}, u32[]{:S(2)}) collective-permute-start(bf16[2,128,448]{1,2,0:T(8,128)(2,1)S(1)} %get-tuple-element.46), channel_id=1, source_target_pairs={{0,2},{1,3},{2,0},{3,1},{4,6},{5,7},{6,4},{7,5},{8,10},{9,11},{10,... | collective-permute-start | bytes 688136 | tf_op jit(solution)/shard_map/ppermute | solution.py:93
  182.0 5.3 %collective-permute-start.11 = (bf16[2,128,448]{1,2,0:T(8,128)(2,1)S(1)}, bf16[2,128,448]{1,2,0:T(8,128)(2,1)S(1)}, u32[]{:S(2)}, u32[]{:S(2)}) collective-permute-start(bf16[2,128,448]{1,2,0:T(8,128)(2,1)S(1)} %get-tuple-element.45), channel_id=1, source_target_pairs={{0,3},{1,2},{2,1},{3,0},{4,7},{5,6},{6,5},{7,4},{8,11},{9,10},{10,... | collective-permute-start | bytes 688136 | tf_op jit(solution)/shard_map/ppermute | solution.py:93
  187.3 2.2 collective-permute-start.9
  189.5 1.3 add_convert_fusion.1
  190.8 5.9 %collective-permute-start.8 = (bf16[128,448]{0,1:T(8,128)(2,1)S(1)}, bf16[128,448]{0,1:T(8,128)(2,1)S(1)}, u32[]{:S(2)}, u32[]{:S(2)}) collective-permute-start(bf16[128,448]{0,1:T(8,128)(2,1)S(1)} %dynamic-slice_bitcast_fusion.10), channel_id=1, source_target_pairs={{0,4},{4,0},{1,5},{5,1},{2,6},{6,2},{3,7},{7,3},{8,12},{12,8},{9,1... | collective-permute-start | bytes 344072 | tf_op jit(solution)/shard_map/ppermute | solution.py:14
  196.8 4.6 %collective-permute-done.10 = bf16[2,128,448]{1,2,0:T(8,128)(2,1)S(1)} collective-permute-done((bf16[2,128,448]{1,2,0:T(8,128)(2,1)S(1)}, bf16[2,128,448]{1,2,0:T(8,128)(2,1)S(1)}, u32[]{:S(2)}, u32[]{:S(2)}) %collective-permute-start.10) | collective-permute-done | bytes 229408 | tf_op jit(solution)/shard_map/ppermute | solution.py:93
  201.3 5.2 %collective-permute-done.9 = bf16[2,128,448]{1,2,0:T(8,128)(2,1)S(1)} collective-permute-done((bf16[2,128,448]{1,2,0:T(8,128)(2,1)S(1)}, bf16[2,128,448]{1,2,0:T(8,128)(2,1)S(1)}, u32[]{:S(2)}, u32[]{:S(2)}) %collective-permute-start.9) | collective-permute-done | bytes 229408 | tf_op jit(solution)/shard_map/ppermute | solution.py:93
  206.6 0.1 add_convert_fusion
  206.7 3.9 %collective-permute-start.12 = (bf16[128,448]{0,1:T(8,128)(2,1)S(1)}, bf16[128,448]{0,1:T(8,128)(2,1)S(1)}, u32[]{:S(2)}, u32[]{:S(2)}) collective-permute-start(bf16[128,448]{0,1:T(8,128)(2,1)S(1)} %get-tuple-element.48), channel_id=1, source_target_pairs={{0,23},{1,22},{2,21},{3,20},{4,19},{5,18},{6,17},{7,16},{16,7},{17... | collective-permute-start | bytes 344072 | tf_op jit(solution)/shard_map/ppermute | solution.py:18
  210.6 6.0 %collective-permute-start.13 = (bf16[128,448]{0,1:T(8,128)(2,1)S(1)}, bf16[128,448]{0,1:T(8,128)(2,1)S(1)}, u32[]{:S(2)}, u32[]{:S(2)}) collective-permute-start(bf16[128,448]{0,1:T(8,128)(2,1)S(1)} %get-tuple-element.49), channel_id=1, source_target_pairs={{0,19},{1,18},{2,17},{3,16},{4,23},{5,22},{6,21},{7,20},{16,3},{17... | collective-permute-start | bytes 344072 | tf_op jit(solution)/shard_map/ppermute | solution.py:160
  216.6 2.6 %collective-permute-done.12 = bf16[128,448]{0,1:T(8,128)(2,1)S(1)} collective-permute-done((bf16[128,448]{0,1:T(8,128)(2,1)S(1)}, bf16[128,448]{0,1:T(8,128)(2,1)S(1)}, u32[]{:S(2)}, u32[]{:S(2)}) %collective-permute-start.12) | collective-permute-done | bytes 114720 | tf_op jit(solution)/shard_map/ppermute | solution.py:18
  219.2 16.3 %collective-permute-done.13 = bf16[128,448]{0,1:T(8,128)(2,1)S(1)} collective-permute-done((bf16[128,448]{0,1:T(8,128)(2,1)S(1)}, bf16[128,448]{0,1:T(8,128)(2,1)S(1)}, u32[]{:S(2)}, u32[]{:S(2)}) %collective-permute-start.13) | collective-permute-done | bytes 114720 | tf_op jit(solution)/shard_map/ppermute | solution.py:160
  235.5 0.7 fusion.52
  236.2 1.1 copy.21
  (40 shorter events, 0.3 us)
Async XLA Ops:
  0.6 7.1 %copy-start.4 = (bf16[128,3584]{1,0:T(8,128)(2,1)S(1)}, bf16[128,3584]{1,0:T(8,128)(2,1)}, u32[]{:S(2)}) copy-start(bf16[128,3584]{1,0:T(8,128)(2,1)} %param.6) | copy-start | bytes 2752516
  0.6 33.0 %all-to-all-start = ((bf16[16,336,128]{2,1,0:T(8,128)(2,1)}), bf16[16,336,128]{2,1,0:T(8,128)(2,1)S(1)}, u32[]{:S(2)}, u32[]{:S(2)}) async-start(bf16[16,336,128]{2,1,0:T(8,128)(2,1)} %bitcast.112), calls=%async_computation | async-start | bytes 2752512 | tf_op jit(solution)/shard_map/all_to_all | solution.py:131
  8.3 13.4 %copy-start.6 = (s32[32]{0:T(128)S(1)}, s32[32]{0:T(128)}, u32[]{:S(2)}) copy-start(s32[32]{0:T(128)} %param.10) | copy-start | bytes 388
  8.3 13.4 %copy-start.7 = (s32[32]{0:T(128)S(1)}, s32[32]{0:T(128)}, u32[]{:S(2)}) copy-start(s32[32]{0:T(128)} %param.11) | copy-start | bytes 388
  8.4 14.0 %copy-start.8 = (s32[128,2]{0,1:T(2,128)S(1)}, s32[128,2]{0,1:T(2,128)}, u32[]{:S(2)}) copy-start(s32[128,2]{0,1:T(2,128)} %param.7) | copy-start | bytes 3076
  8.4 14.2 %copy-start.5 = (f32[128,2]{0,1:T(2,128)S(1)}, f32[128,2]{0,1:T(2,128)}, u32[]{:S(2)}) copy-start(f32[128,2]{0,1:T(2,128)} %param.8) | copy-start | bytes 3076
  10.6 23.0 %collective-permute-start = (bf16[64,1792]{1,0:T(8,128)(2,1)S(1)}, bf16[64,1792]{1,0:T(8,128)(2,1)S(1)}, u32[]{:S(2)}, u32[]{:S(2)}) collective-permute-start(bf16[64,1792]{1,0:T(8,128)(2,1)S(1)} %constant_dynamic-slice_fusion), channel_id=1, source_target_pairs={{0,23},{1,22},{2,21},{3,20},{4,19},{5,18},{6,17},{7,16},{16,7},{17... | collective-permute-start | bytes 688136 | tf_op jit(solution)/shard_map/ppermute | solution.py:18
  22.6 11.0 %collective-permute-start.1 = (f32[4,128]{1,0:T(4,128)S(1)}, f32[4,128]{1,0:T(4,128)S(1)}, u32[]{:S(2)}, u32[]{:S(2)}) collective-permute-start(f32[4,128]{1,0:T(4,128)S(1)} %pad_maximum_fusion), channel_id=1, source_target_pairs={{0,23},{1,22},{2,21},{3,20},{4,19},{5,18},{6,17},{7,16},{16,7},{17... | collective-permute-start | bytes 6152 | tf_op jit(solution)/shard_map/ppermute | solution.py:18
  33.6 34.1 %all-to-all-start.1 = ((bf16[32,16,1792]{2,1,0:T(8,128)(2,1)}), bf16[32,16,1792]{2,1,0:T(8,128)(2,1)S(1)}, u32[]{:S(2)}, u32[]{:S(2)}) async-start(bf16[32,16,1792]{2,1,0:T(8,128)(2,1)} %bitcast.16), calls=%async_computation.1 | async-start | bytes 3670016 | tf_op jit(solution)/shard_map/all_to_all | solution.py:57
  67.7 1.3 copy-start.3
  69.0 21.4 %copy-start.2 = (bf16[1,3,1792,128]{3,2,1,0:T(8,128)(2,1)S(1)}, bf16[1,3,1792,128]{3,2,1,0:T(8,128)(2,1)}, u32[]{:S(2)}) copy-start(bf16[1,3,1792,128]{3,2,1,0:T(8,128)(2,1)} %param.9) | copy-start | bytes 4128772
  69.0 33.0 %all-to-all-start.2 = ((bf16[32,16,1792]{2,1,0:T(8,128)(2,1)}), bf16[32,16,1792]{2,1,0:T(8,128)(2,1)}, u32[]{:S(2)}, u32[]{:S(2)}) async-start(bf16[32,16,1792]{2,1,0:T(8,128)(2,1)} %bitcast.23), calls=%async_computation.2 | async-start | bytes 3670016 | tf_op jit(solution)/shard_map/all_to_all | solution.py:57
  81.5 14.4 %collective-permute-start.3 = (bf16[336,128]{1,0:T(8,128)(2,1)S(1)}, bf16[336,128]{1,0:T(8,128)(2,1)S(1)}, u32[]{:S(2)}, u32[]{:S(2)}) collective-permute-start(bf16[336,128]{1,0:T(8,128)(2,1)S(1)} %bitcast_select_fusion.1), channel_id=1, source_target_pairs={{0,16},{16,0},{1,17},{17,1},{2,18},{18,2},{3,19},{19,3},{4,20},{20... | collective-permute-start | bytes 258056 | tf_op jit(solution)/shard_map/ppermute | solution.py:14
  92.6 4.7 %collective-permute-start.2 = (f32[2,512,128]{2,1,0:T(8,128)S(1)}, f32[2,512,128]{2,1,0:T(8,128)S(1)}, u32[]{:S(2)}, u32[]{:S(2)}) collective-permute-start(f32[2,512,128]{2,1,0:T(8,128)S(1)} %fusion.6), channel_id=1, source_target_pairs={{0,8},{8,0},{1,9},{9,1},{2,10},{10,2},{3,11},{11,3},{4,12},{12,4},... | collective-permute-start | bytes 1572872 | tf_op jit(solution)/shard_map/ppermute | solution.py:14
  102.0 31.8 %all-to-all-start.3 = ((bf16[32,16,1792]{2,1,0:T(8,128)(2,1)}), bf16[32,16,1792]{2,1,0:T(8,128)(2,1)S(1)}, u32[]{:S(2)}, u32[]{:S(2)}) async-start(bf16[32,16,1792]{2,1,0:T(8,128)(2,1)} %bitcast.110), calls=%async_computation.3 | async-start | bytes 3670016 | tf_op jit(solution)/shard_map/all_to_all | solution.py:57
  111.6 3.8 %collective-permute-start.4 = (f32[2,512,128]{2,1,0:T(8,128)S(1)}, f32[2,512,128]{2,1,0:T(8,128)S(1)}, u32[]{:S(2)}, u32[]{:S(2)}) collective-permute-start(f32[2,512,128]{2,1,0:T(8,128)S(1)} %fusion.9), channel_id=1, source_target_pairs={{0,8},{8,0},{1,9},{9,1},{2,10},{10,2},{3,11},{11,3},{4,12},{12,4},... | collective-permute-start | bytes 1572872 | tf_op jit(solution)/shard_map/ppermute | solution.py:14
  133.8 1.2 copy-start
  135.0 32.5 %all-to-all-start.4 = ((bf16[32,16,1792]{2,1,0:T(8,128)(2,1)}), bf16[32,16,1792]{2,1,0:T(8,128)(2,1)S(1)}, u32[]{:S(2)}, u32[]{:S(2)}) async-start(bf16[32,16,1792]{2,1,0:T(8,128)(2,1)} %bitcast.109), calls=%async_computation.4 | async-start | bytes 3670016 | tf_op jit(solution)/shard_map/all_to_all | solution.py:57
  141.6 2.4 %copy-start.1 = (bf16[32,16,1792]{2,1,0:T(8,128)(2,1)S(1)}, bf16[32,16,1792]{2,1,0:T(8,128)(2,1)}, u32[]{:S(2)}) copy-start(bf16[32,16,1792]{2,1,0:T(8,128)(2,1)} %copy-done) | copy-start | bytes 5505028
  153.5 33.8 %collective-permute-start.5 = (bf16[2,128,448]{1,2,0:T(8,128)(2,1)}, bf16[2,128,448]{1,2,0:T(8,128)(2,1)}, u32[]{:S(2)}, u32[]{:S(2)}) collective-permute-start(bf16[2,128,448]{1,2,0:T(8,128)(2,1)} %get-tuple-element.40), channel_id=1, source_target_pairs={{0,1},{1,0},{2,3},{3,2},{4,5},{5,4},{6,7},{7,6},{8,9},{9,8},{10,11... | collective-permute-start | bytes 688136 | tf_op jit(solution)/shard_map/ppermute | solution.py:93
  155.5 34.1 %collective-permute-start.6 = (bf16[2,128,448]{1,2,0:T(8,128)(2,1)S(1)}, bf16[2,128,448]{1,2,0:T(8,128)(2,1)}, u32[]{:S(2)}, u32[]{:S(2)}) collective-permute-start(bf16[2,128,448]{1,2,0:T(8,128)(2,1)S(1)} %get-tuple-element.42), channel_id=1, source_target_pairs={{0,2},{1,3},{2,0},{3,1},{4,6},{5,7},{6,4},{7,5},{8,10},{9,11},{10,... | collective-permute-start | bytes 688136 | tf_op jit(solution)/shard_map/ppermute | solution.py:93
  165.5 24.0 %collective-permute-start.7 = (bf16[2,128,448]{1,2,0:T(8,128)(2,1)S(1)}, bf16[2,128,448]{1,2,0:T(8,128)(2,1)}, u32[]{:S(2)}, u32[]{:S(2)}) collective-permute-start(bf16[2,128,448]{1,2,0:T(8,128)(2,1)S(1)} %get-tuple-element.41), channel_id=1, source_target_pairs={{0,3},{1,2},{2,1},{3,0},{4,7},{5,6},{6,5},{7,4},{8,11},{9,10},{10,... | collective-permute-start | bytes 688136 | tf_op jit(solution)/shard_map/ppermute | solution.py:93
  172.1 64.1 %all-to-all-start.5 = ((bf16[16,336,128]{2,1,0:T(8,128)(2,1)}), bf16[16,336,128]{2,1,0:T(8,128)(2,1)S(1)}, u32[]{:S(2)}, u32[]{:S(2)}) async-start(bf16[16,336,128]{2,1,0:T(8,128)(2,1)} %select_select_fusion), calls=%async_computation.5 | async-start | bytes 2752512 | tf_op jit(solution)/shard_map/all_to_all | solution.py:152
  178.9 22.4 %collective-permute-start.10 = (bf16[2,128,448]{1,2,0:T(8,128)(2,1)S(1)}, bf16[2,128,448]{1,2,0:T(8,128)(2,1)S(1)}, u32[]{:S(2)}, u32[]{:S(2)}) collective-permute-start(bf16[2,128,448]{1,2,0:T(8,128)(2,1)S(1)} %get-tuple-element.46), channel_id=1, source_target_pairs={{0,2},{1,3},{2,0},{3,1},{4,6},{5,7},{6,4},{7,5},{8,10},{9,11},{10,... | collective-permute-start | bytes 688136 | tf_op jit(solution)/shard_map/ppermute | solution.py:93
  182.0 19.3 %collective-permute-start.11 = (bf16[2,128,448]{1,2,0:T(8,128)(2,1)S(1)}, bf16[2,128,448]{1,2,0:T(8,128)(2,1)S(1)}, u32[]{:S(2)}, u32[]{:S(2)}) collective-permute-start(bf16[2,128,448]{1,2,0:T(8,128)(2,1)S(1)} %get-tuple-element.45), channel_id=1, source_target_pairs={{0,3},{1,2},{2,1},{3,0},{4,7},{5,6},{6,5},{7,4},{8,11},{9,10},{10,... | collective-permute-start | bytes 688136 | tf_op jit(solution)/shard_map/ppermute | solution.py:93
  187.3 19.2 %collective-permute-start.9 = (bf16[2,128,448]{1,2,0:T(8,128)(2,1)S(1)}, bf16[2,128,448]{1,2,0:T(8,128)(2,1)S(1)}, u32[]{:S(2)}, u32[]{:S(2)}) collective-permute-start(bf16[2,128,448]{1,2,0:T(8,128)(2,1)S(1)} %get-tuple-element.47), channel_id=1, source_target_pairs={{0,1},{1,0},{2,3},{3,2},{4,5},{5,4},{6,7},{7,6},{8,9},{9,8},{10,11... | collective-permute-start | bytes 688136 | tf_op jit(solution)/shard_map/ppermute | solution.py:93
  190.8 25.7 %collective-permute-start.8 = (bf16[128,448]{0,1:T(8,128)(2,1)S(1)}, bf16[128,448]{0,1:T(8,128)(2,1)S(1)}, u32[]{:S(2)}, u32[]{:S(2)}) collective-permute-start(bf16[128,448]{0,1:T(8,128)(2,1)S(1)} %dynamic-slice_bitcast_fusion.10), channel_id=1, source_target_pairs={{0,4},{4,0},{1,5},{5,1},{2,6},{6,2},{3,7},{7,3},{8,12},{12,8},{9,1... | collective-permute-start | bytes 344072 | tf_op jit(solution)/shard_map/ppermute | solution.py:14
  206.7 12.4 %collective-permute-start.12 = (bf16[128,448]{0,1:T(8,128)(2,1)S(1)}, bf16[128,448]{0,1:T(8,128)(2,1)S(1)}, u32[]{:S(2)}, u32[]{:S(2)}) collective-permute-start(bf16[128,448]{0,1:T(8,128)(2,1)S(1)} %get-tuple-element.48), channel_id=1, source_target_pairs={{0,23},{1,22},{2,21},{3,20},{4,19},{5,18},{6,17},{7,16},{16,7},{17... | collective-permute-start | bytes 344072 | tf_op jit(solution)/shard_map/ppermute | solution.py:18
  210.6 24.9 %collective-permute-start.13 = (bf16[128,448]{0,1:T(8,128)(2,1)S(1)}, bf16[128,448]{0,1:T(8,128)(2,1)S(1)}, u32[]{:S(2)}, u32[]{:S(2)}) collective-permute-start(bf16[128,448]{0,1:T(8,128)(2,1)S(1)} %get-tuple-element.49), channel_id=1, source_target_pairs={{0,19},{1,18},{2,17},{3,16},{4,23},{5,22},{6,21},{7,20},{16,3},{17... | collective-permute-start | bytes 344072 | tf_op jit(solution)/shard_map/ppermute | solution.py:160
where the time goes:
time: 238 us; the launch traced here: 237 us
  starting transfers between devices  113 us (47%)
  waiting for transfers between devices  58.2 us (24%)
  blocking collectives  21.5 us (9%)
  matrix products  17.6 us (7%)
  local copies, waits for them, and re-layouts  17.5 us (7%)
  other arithmetic  5.65 us (2%)
  between operations  3.79 us (2%)
    all_to_all x4, starting transfers between devices, exchange(): lax.all_to_all(blocks, axes, split_axis=0, concat_axis=0, tiled=True)  32.3 us
    ppermute x6, starting transfers between devices, near_sum(): lax.ppermute(block, NEAR, [(i, i ^ step) for i in range(count)])  24.5 us
    all_gather x1, blocking collectives, shards(): other_table = lax.all_gather(quarter, NEAR, tiled=True)  21.5 us
    all_to_all x4, waiting for transfers between devices, exchange(): lax.all_to_all(blocks, axes, split_axis=0, concat_axis=0, tiled=True)  20 us
    ppermute x4, starting transfers between devices, swap(): return lax.ppermute(value, axis, [(0, 1), (1, 0)])  19.6 us
    ppermute x3, starting transfers between devices, mirrored(): return lax.ppermute(value, RING, [(i, 15 - i) for i in range(16)])  16.9 us
    ppermute x1, waiting for transfers between devices, shards(): lax.ppermute(of(other_kept, far), RING, [(i, i ^ 11) for i in range(16)])  16.3 us
    ppermute x6, waiting for transfers between devices, near_sum(): lax.ppermute(block, NEAR, [(i, i ^ step) for i in range(count)])  9.81 us
  transfers between devices with their start and end apart: 20, of which 10 were waited for; matrix products, arithmetic and copies ran while one was open for 16% of the time, Pallas kernels for 0%

commit v1 on v0

--- a/solution.py
+++ b/solution.py
@@ -137,7 +137,9 @@
     )
     sent = exchange(payload)
     other_rows = placed_rows(other_codes, zh)
-    other_table = lax.all_gather(quarter, NEAR, tiled=True)
+    other_table = jnp.concatenate(
+        lax.all_to_all(jnp.stack([quarter] * lax.axis_size(NEAR)), NEAR, 0, 0), axis=0
+    )
     payload, sent = tied((gather_rows(other_rows, other_table), sent))
     other_sent = exchange(payload)
     chosen = pick_pieces(spread, old_owner, new_owner, zh)

time: 238 us -> 262 us (1.10)
  waiting for transfers between devices: 58.2 us -> 83.3 us
  blocking collectives: 21.5 us -> 30.6 us
  starting transfers between devices: 113 us -> 104 us
    all_to_all x0 -> x1, blocking collectives: none -> 30.6 us  [shards(): lax.all_to_all(jnp.stack([quarter] * lax.axis_size(NEAR)), NEAR, 0, 0)]
    all_to_all x4, waiting for transfers between devices: 20 us -> 42.8 us  [exchange(): lax.all_to_all(blocks, axes, split_axis=0, concat_axis=0, tiled=True)]
    all_gather x1 -> x0, blocking collectives: 21.5 us -> none  [shards(): other_table = lax.all_gather(quarter, NEAR, tiled=True)]
    all_to_all x4, starting transfers between devices: 32.3 us -> 28.5 us  [exchange(): lax.all_to_all(blocks, axes, split_axis=0, concat_axis=0, tiled=True)]
  transfers between devices with their start and end apart: 20 -> 20, of which waited for: 10 -> 11; matrix products, arithmetic and copies ran while one was open for 16% -> 14% of each run, Pallas kernels for 0% -> 0%
where the time goes in v1:
time: 262 us; the launch traced here: 261 us
  starting transfers between devices  104 us (40%)
  waiting for transfers between devices  83.3 us (32%)
  blocking collectives  30.6 us (12%)
  matrix products  17.6 us (7%)
  local copies, waits for them, and re-layouts  16.2 us (6%)
  other arithmetic  5.65 us (2%)
  between operations  3.78 us (1%)
    all_to_all x4, waiting for transfers between devices, exchange(): lax.all_to_all(blocks, axes, split_axis=0, concat_axis=0, tiled=True)  42.8 us
    all_to_all x1, blocking collectives, shards(): lax.all_to_all(jnp.stack([quarter] * lax.axis_size(NEAR)), NEAR, 0, 0)  30.6 us
    all_to_all x4, starting transfers between devices, exchange(): lax.all_to_all(blocks, axes, split_axis=0, concat_axis=0, tiled=True)  28.5 us
    ppermute x6, starting transfers between devices, near_sum(): lax.ppermute(block, NEAR, [(i, i ^ step) for i in range(count)])  22 us
    ppermute x3, starting transfers between devices, mirrored(): return lax.ppermute(value, RING, [(i, 15 - i) for i in range(16)])  18.8 us
    ppermute x4, starting transfers between devices, swap(): return lax.ppermute(value, axis, [(0, 1), (1, 0)])  18.1 us
    ppermute x1, waiting for transfers between devices, shards(): lax.ppermute(of(other_kept, far), RING, [(i, i ^ 11) for i in range(16)])  15.6 us
    ppermute x6, waiting for transfers between devices, near_sum(): lax.ppermute(block, NEAR, [(i, i ^ step) for i in range(count)])  11.4 us
  transfers between devices with their start and end apart: 20, of which 11 were waited for; matrix products, arithmetic and copies ran while one was open for 14% of the time, Pallas kernels for 0%

profile of v1, /device:TPU:99, one launch (start us, length us, event | category | flops | bytes accessed | tf_op | source)
XLA Modules:
  0.0 260.9 jit_solution(18120433896649765108)
XLA Ops:
  0.6 7.1 %all-to-all-start = ((bf16[16,336,128]{2,1,0:T(8,128)(2,1)}), bf16[16,336,128]{2,1,0:T(8,128)(2,1)S(1)}, u32[]{:S(2)}, u32[]{:S(2)}) async-start(bf16[16,336,128]{2,1,0:T(8,128)(2,1)} %bitcast.113), calls=%async_computation | async-start | bytes 2752512 | tf_op jit(solution)/shard_map/all_to_all | solution.py:131
  7.7 0.6 copy.9
  8.4 0.9 copy.16
  9.3 1.3 reshape.280
  10.6 11.1 %collective-permute-start = (bf16[64,1792]{1,0:T(8,128)(2,1)S(1)}, bf16[64,1792]{1,0:T(8,128)(2,1)S(1)}, u32[]{:S(2)}, u32[]{:S(2)}) collective-permute-start(bf16[64,1792]{1,0:T(8,128)(2,1)S(1)} %constant_dynamic-slice_fusion), channel_id=1, source_target_pairs={{0,23},{1,22},{2,21},{3,20},{4,19},{5,18},{6,17},{7,16},{16,7},{17... | collective-permute-start | bytes 688136 | tf_op jit(solution)/shard_map/ppermute | solution.py:18
  21.7 0.6 fusion.67
  22.4 0.2 fusion.13
  22.6 1.9 collective-permute-start.1
  24.6 1.9 convolution_convert_fusion.1
  26.5 7.1 %collective-permute-done.1 = f32[4,128]{1,0:T(4,128)S(1)} collective-permute-done((f32[4,128]{1,0:T(4,128)S(1)}, f32[4,128]{1,0:T(4,128)S(1)}, u32[]{:S(2)}, u32[]{:S(2)}) %collective-permute-start.1) | collective-permute-done | bytes 2080 | tf_op jit(solution)/shard_map/ppermute | solution.py:18
  33.6 0.1 stack.25
  33.7 30.6 %all_to_all.35 = bf16[4,64,1792]{2,1,0:T(8,128)(2,1)S(1)} all-to-all(bf16[4,64,1792]{2,1,0:T(8,128)(2,1)S(1)} %stack.25), channel_id=1, replica_groups=mesh['y'=4,'x'=4,'zh'=2,'c'=2,'ma'=2,'mb'=2,'mc'=2] {'mb','mc'}, dimensions={0} | all-to-all | bytes 1835008 | tf_op jit(solution)/shard_map/all_to_all | solution.py:141
  64.3 8.2 %all-to-all-start.2 = ((bf16[32,16,1792]{2,1,0:T(8,128)(2,1)}), bf16[32,16,1792]{2,1,0:T(8,128)(2,1)}, u32[]{:S(2)}, u32[]{:S(2)}) async-start(bf16[32,16,1792]{2,1,0:T(8,128)(2,1)} %bitcast.17), calls=%async_computation.2 | async-start | bytes 3670016 | tf_op jit(solution)/shard_map/all_to_all | solution.py:57
  72.5 1.9 convolution_convert_fusion
  74.4 22.5 %all-to-all-done.2 = bf16[32,16,1792]{2,1,0:T(8,128)(2,1)} async-done(((bf16[32,16,1792]{2,1,0:T(8,128)(2,1)}), bf16[32,16,1792]{2,1,0:T(8,128)(2,1)}, u32[]{:S(2)}, u32[]{:S(2)}) %all-to-all-start.2) | async-done | bytes 1835040 | tf_op jit(solution)/shard_map/all_to_all | solution.py:57
  96.9 7.3 %all-to-all-start.3 = ((bf16[32,16,1792]{2,1,0:T(8,128)(2,1)}), bf16[32,16,1792]{2,1,0:T(8,128)(2,1)}, u32[]{:S(2)}, u32[]{:S(2)}) async-start(bf16[32,16,1792]{2,1,0:T(8,128)(2,1)} %bitcast.24), calls=%async_computation.3 | async-start | bytes 3670016 | tf_op jit(solution)/shard_map/all_to_all | solution.py:57
  106.8 1.3 fusion.69
  108.1 8.0 %collective-permute-start.3 = (bf16[336,128]{1,0:T(8,128)(2,1)S(1)}, bf16[336,128]{1,0:T(8,128)(2,1)S(1)}, u32[]{:S(2)}, u32[]{:S(2)}) collective-permute-start(bf16[336,128]{1,0:T(8,128)(2,1)S(1)} %bitcast_select_fusion.1), channel_id=1, source_target_pairs={{0,16},{16,0},{1,17},{17,1},{2,18},{18,2},{3,19},{19,3},{4,20},{20... | collective-permute-start | bytes 258056 | tf_op jit(solution)/shard_map/ppermute | solution.py:14
  116.1 2.1 fusion.6
  118.2 2.5 collective-permute-start.2
  120.8 1.7 collective-permute-done.3
  122.5 1.3 select_select_fusion
  123.9 1.9 convolution_convert_fusion.3
  125.8 2.9 %all-to-all-done.3 = bf16[32,16,1792]{2,1,0:T(8,128)(2,1)} async-done(((bf16[32,16,1792]{2,1,0:T(8,128)(2,1)}), bf16[32,16,1792]{2,1,0:T(8,128)(2,1)}, u32[]{:S(2)}, u32[]{:S(2)}) %all-to-all-start.3) | async-done | bytes 1835040 | tf_op jit(solution)/shard_map/all_to_all | solution.py:57
  128.7 6.5 %all-to-all-start.4 = ((bf16[32,16,1792]{2,1,0:T(8,128)(2,1)}), bf16[32,16,1792]{2,1,0:T(8,128)(2,1)S(1)}, u32[]{:S(2)}, u32[]{:S(2)}) async-start(bf16[32,16,1792]{2,1,0:T(8,128)(2,1)} %bitcast.111), calls=%async_computation.4 | async-start | bytes 3670016 | tf_op jit(solution)/shard_map/all_to_all | solution.py:57
  135.2 2.1 fusion.9
  137.3 2.3 collective-permute-start.4
  139.6 1.5 collective-permute-done.4
  141.1 0.1 add.237
  141.2 1.9 convolution_convert_fusion.2
  143.1 16.5 %all-to-all-done.4 = bf16[32,16,1792]{2,1,0:T(8,128)(2,1)S(1)} async-done(((bf16[32,16,1792]{2,1,0:T(8,128)(2,1)}), bf16[32,16,1792]{2,1,0:T(8,128)(2,1)S(1)}, u32[]{:S(2)}, u32[]{:S(2)}) %all-to-all-start.4) | async-done | bytes 1835040 | tf_op jit(solution)/shard_map/all_to_all | solution.py:57
  159.6 1.2 copy-done
  160.8 6.5 %all-to-all-start.5 = ((bf16[32,16,1792]{2,1,0:T(8,128)(2,1)}), bf16[32,16,1792]{2,1,0:T(8,128)(2,1)S(1)}, u32[]{:S(2)}, u32[]{:S(2)}) async-start(bf16[32,16,1792]{2,1,0:T(8,128)(2,1)} %bitcast.110), calls=%async_computation.5 | async-start | bytes 3670016 | tf_op jit(solution)/shard_map/all_to_all | solution.py:57
  167.4 2.4 fusion.45
  169.8 1.7 fusion
  171.5 3.5 %reshape.281 = bf16[2,128,2,4,224]{4,3,2,1,0:T(4,128)(2,1)S(1)} reshape(bf16[256,1792]{1,0:T(8,128)(2,1)} %fusion) | data formatting | bytes 1835008 | tf_op jit(solution)/shard_map/reshape | solution.py:82
  175.0 2.3 copy.18
  177.3 1.3 copy.13
  178.6 0.8 dynamic-slice_bitcast_fusion.6
  179.3 1.9 collective-permute-start.5
  181.3 7.6 %collective-permute-start.6 = (bf16[2,128,448]{1,2,0:T(8,128)(2,1)S(1)}, bf16[2,128,448]{1,2,0:T(8,128)(2,1)}, u32[]{:S(2)}, u32[]{:S(2)}) collective-permute-start(bf16[2,128,448]{1,2,0:T(8,128)(2,1)S(1)} %get-tuple-element.42), channel_id=1, source_target_pairs={{0,2},{1,3},{2,0},{3,1},{4,6},{5,7},{6,4},{7,5},{8,10},{9,11},{10,... | collective-permute-start | bytes 688136 | tf_op jit(solution)/shard_map/ppermute | solution.py:93
  188.9 1.9 collective-permute-start.7
  190.8 0.9 all-to-all-done.5
  191.7 0.8 fusion.48
  192.5 0.8 fusion.1
  193.3 1.5 reshape.282
  194.7 1.4 copy.19
  196.2 0.1 copy.15
  196.3 0.1 dynamic-slice_bitcast_fusion.3
  196.4 5.9 %all-to-all-start.6 = ((bf16[16,336,128]{2,1,0:T(8,128)(2,1)}), bf16[16,336,128]{2,1,0:T(8,128)(2,1)S(1)}, u32[]{:S(2)}, u32[]{:S(2)}) async-start(bf16[16,336,128]{2,1,0:T(8,128)(2,1)} %select_select_fusion), calls=%async_computation.6 | async-start | bytes 2752512 | tf_op jit(solution)/shard_map/all_to_all | solution.py:154
  202.2 5.4 %collective-permute-start.10 = (bf16[2,128,448]{1,2,0:T(8,128)(2,1)S(1)}, bf16[2,128,448]{1,2,0:T(8,128)(2,1)S(1)}, u32[]{:S(2)}, u32[]{:S(2)}) collective-permute-start(bf16[2,128,448]{1,2,0:T(8,128)(2,1)S(1)} %get-tuple-element.46), channel_id=1, source_target_pairs={{0,2},{1,3},{2,0},{3,1},{4,6},{5,7},{6,4},{7,5},{8,10},{9,11},{10,... | collective-permute-start | bytes 688136 | tf_op jit(solution)/shard_map/ppermute | solution.py:93
  207.6 3.1 %collective-permute-start.11 = (bf16[2,128,448]{1,2,0:T(8,128)(2,1)S(1)}, bf16[2,128,448]{1,2,0:T(8,128)(2,1)S(1)}, u32[]{:S(2)}, u32[]{:S(2)}) collective-permute-start(bf16[2,128,448]{1,2,0:T(8,128)(2,1)S(1)} %get-tuple-element.45), channel_id=1, source_target_pairs={{0,3},{1,2},{2,1},{3,0},{4,7},{5,6},{6,5},{7,4},{8,11},{9,10},{10,... | collective-permute-start | bytes 688136 | tf_op jit(solution)/shard_map/ppermute | solution.py:93
  210.7 2.2 collective-permute-start.9
  212.9 1.3 add_convert_fusion.1
  214.2 5.3 %collective-permute-start.8 = (bf16[128,448]{0,1:T(8,128)(2,1)S(1)}, bf16[128,448]{0,1:T(8,128)(2,1)S(1)}, u32[]{:S(2)}, u32[]{:S(2)}) collective-permute-start(bf16[128,448]{0,1:T(8,128)(2,1)S(1)} %dynamic-slice_bitcast_fusion.10), channel_id=1, source_target_pairs={{0,4},{4,0},{1,5},{5,1},{2,6},{6,2},{3,7},{7,3},{8,12},{12,8},{9,1... | collective-permute-start | bytes 344072 | tf_op jit(solution)/shard_map/ppermute | solution.py:14
  219.6 4.7 %collective-permute-done.10 = bf16[2,128,448]{1,2,0:T(8,128)(2,1)S(1)} collective-permute-done((bf16[2,128,448]{1,2,0:T(8,128)(2,1)S(1)}, bf16[2,128,448]{1,2,0:T(8,128)(2,1)S(1)}, u32[]{:S(2)}, u32[]{:S(2)}) %collective-permute-start.10) | collective-permute-done | bytes 229408 | tf_op jit(solution)/shard_map/ppermute | solution.py:93
  224.2 6.7 %collective-permute-done.9 = bf16[2,128,448]{1,2,0:T(8,128)(2,1)S(1)} collective-permute-done((bf16[2,128,448]{1,2,0:T(8,128)(2,1)S(1)}, bf16[2,128,448]{1,2,0:T(8,128)(2,1)S(1)}, u32[]{:S(2)}, u32[]{:S(2)}) %collective-permute-start.9) | collective-permute-done | bytes 229408 | tf_op jit(solution)/shard_map/ppermute | solution.py:93
  230.9 0.1 add_convert_fusion
  231.1 5.8 %collective-permute-start.12 = (bf16[128,448]{0,1:T(8,128)(2,1)S(1)}, bf16[128,448]{0,1:T(8,128)(2,1)S(1)}, u32[]{:S(2)}, u32[]{:S(2)}) collective-permute-start(bf16[128,448]{0,1:T(8,128)(2,1)S(1)} %get-tuple-element.48), channel_id=1, source_target_pairs={{0,23},{1,22},{2,21},{3,20},{4,19},{5,18},{6,17},{7,16},{16,7},{17... | collective-permute-start | bytes 344072 | tf_op jit(solution)/shard_map/ppermute | solution.py:18
  236.8 3.4 %collective-permute-start.13 = (bf16[128,448]{0,1:T(8,128)(2,1)S(1)}, bf16[128,448]{0,1:T(8,128)(2,1)S(1)}, u32[]{:S(2)}, u32[]{:S(2)}) collective-permute-start(bf16[128,448]{0,1:T(8,128)(2,1)S(1)} %get-tuple-element.49), channel_id=1, source_target_pairs={{0,19},{1,18},{2,17},{3,16},{4,23},{5,22},{6,21},{7,20},{16,3},{17... | collective-permute-start | bytes 344072 | tf_op jit(solution)/shard_map/ppermute | solution.py:162
  240.2 3.3 %collective-permute-done.12 = bf16[128,448]{0,1:T(8,128)(2,1)S(1)} collective-permute-done((bf16[128,448]{0,1:T(8,128)(2,1)S(1)}, bf16[128,448]{0,1:T(8,128)(2,1)S(1)}, u32[]{:S(2)}, u32[]{:S(2)}) %collective-permute-start.12) | collective-permute-done | bytes 114720 | tf_op jit(solution)/shard_map/ppermute | solution.py:18
  243.5 15.6 %collective-permute-done.13 = bf16[128,448]{0,1:T(8,128)(2,1)S(1)} collective-permute-done((bf16[128,448]{0,1:T(8,128)(2,1)S(1)}, bf16[128,448]{0,1:T(8,128)(2,1)S(1)}, u32[]{:S(2)}, u32[]{:S(2)}) %collective-permute-start.13) | collective-permute-done | bytes 114720 | tf_op jit(solution)/shard_map/ppermute | solution.py:162
  259.1 0.7 fusion.52
  259.8 1.1 copy.21
  (39 shorter events, 0.3 us)
Async XLA Ops:
  0.6 7.1 %copy-start.3 = (bf16[128,3584]{1,0:T(8,128)(2,1)S(1)}, bf16[128,3584]{1,0:T(8,128)(2,1)}, u32[]{:S(2)}) copy-start(bf16[128,3584]{1,0:T(8,128)(2,1)} %param.6) | copy-start | bytes 2752516
  0.6 33.0 %all-to-all-start = ((bf16[16,336,128]{2,1,0:T(8,128)(2,1)}), bf16[16,336,128]{2,1,0:T(8,128)(2,1)S(1)}, u32[]{:S(2)}, u32[]{:S(2)}) async-start(bf16[16,336,128]{2,1,0:T(8,128)(2,1)} %bitcast.113), calls=%async_computation | async-start | bytes 2752512 | tf_op jit(solution)/shard_map/all_to_all | solution.py:131
  8.3 13.4 %copy-start.5 = (s32[32]{0:T(128)S(1)}, s32[32]{0:T(128)}, u32[]{:S(2)}) copy-start(s32[32]{0:T(128)} %param.10) | copy-start | bytes 388
  8.3 13.4 %copy-start.6 = (s32[32]{0:T(128)S(1)}, s32[32]{0:T(128)}, u32[]{:S(2)}) copy-start(s32[32]{0:T(128)} %param.11) | copy-start | bytes 388
  8.4 14.0 %copy-start.7 = (s32[128,2]{0,1:T(2,128)S(1)}, s32[128,2]{0,1:T(2,128)}, u32[]{:S(2)}) copy-start(s32[128,2]{0,1:T(2,128)} %param.7) | copy-start | bytes 3076
  8.4 14.2 %copy-start.4 = (f32[128,2]{0,1:T(2,128)S(1)}, f32[128,2]{0,1:T(2,128)}, u32[]{:S(2)}) copy-start(f32[128,2]{0,1:T(2,128)} %param.8) | copy-start | bytes 3076
  10.6 23.0 %collective-permute-start = (bf16[64,1792]{1,0:T(8,128)(2,1)S(1)}, bf16[64,1792]{1,0:T(8,128)(2,1)S(1)}, u32[]{:S(2)}, u32[]{:S(2)}) collective-permute-start(bf16[64,1792]{1,0:T(8,128)(2,1)S(1)} %constant_dynamic-slice_fusion), channel_id=1, source_target_pairs={{0,23},{1,22},{2,21},{3,20},{4,19},{5,18},{6,17},{7,16},{16,7},{17... | collective-permute-start | bytes 688136 | tf_op jit(solution)/shard_map/ppermute | solution.py:18
  22.6 11.0 %collective-permute-start.1 = (f32[4,128]{1,0:T(4,128)S(1)}, f32[4,128]{1,0:T(4,128)S(1)}, u32[]{:S(2)}, u32[]{:S(2)}) collective-permute-start(f32[4,128]{1,0:T(4,128)S(1)} %pad_maximum_fusion), channel_id=1, source_target_pairs={{0,23},{1,22},{2,21},{3,20},{4,19},{5,18},{6,17},{7,16},{16,7},{17... | collective-permute-start | bytes 6152 | tf_op jit(solution)/shard_map/ppermute | solution.py:18
  64.3 32.6 %all-to-all-start.2 = ((bf16[32,16,1792]{2,1,0:T(8,128)(2,1)}), bf16[32,16,1792]{2,1,0:T(8,128)(2,1)}, u32[]{:S(2)}, u32[]{:S(2)}) async-start(bf16[32,16,1792]{2,1,0:T(8,128)(2,1)} %bitcast.17), calls=%async_computation.2 | async-start | bytes 3670016 | tf_op jit(solution)/shard_map/all_to_all | solution.py:57
  96.9 19.2 %copy-start.2 = (bf16[1,3,1792,128]{3,2,1,0:T(8,128)(2,1)S(1)}, bf16[1,3,1792,128]{3,2,1,0:T(8,128)(2,1)}, u32[]{:S(2)}) copy-start(bf16[1,3,1792,128]{3,2,1,0:T(8,128)(2,1)} %param.9) | copy-start | bytes 4128772
  96.9 31.8 %all-to-all-start.3 = ((bf16[32,16,1792]{2,1,0:T(8,128)(2,1)}), bf16[32,16,1792]{2,1,0:T(8,128)(2,1)}, u32[]{:S(2)}, u32[]{:S(2)}) async-start(bf16[32,16,1792]{2,1,0:T(8,128)(2,1)} %bitcast.24), calls=%async_computation.3 | async-start | bytes 3670016 | tf_op jit(solution)/shard_map/all_to_all | solution.py:57
  108.1 14.4 %collective-permute-start.3 = (bf16[336,128]{1,0:T(8,128)(2,1)S(1)}, bf16[336,128]{1,0:T(8,128)(2,1)S(1)}, u32[]{:S(2)}, u32[]{:S(2)}) collective-permute-start(bf16[336,128]{1,0:T(8,128)(2,1)S(1)} %bitcast_select_fusion.1), channel_id=1, source_target_pairs={{0,16},{16,0},{1,17},{17,1},{2,18},{18,2},{3,19},{19,3},{4,20},{20... | collective-permute-start | bytes 258056 | tf_op jit(solution)/shard_map/ppermute | solution.py:14
  118.2 5.6 %collective-permute-start.2 = (f32[2,512,128]{2,1,0:T(8,128)S(1)}, f32[2,512,128]{2,1,0:T(8,128)S(1)}, u32[]{:S(2)}, u32[]{:S(2)}) collective-permute-start(f32[2,512,128]{2,1,0:T(8,128)S(1)} %fusion.6), channel_id=1, source_target_pairs={{0,8},{8,0},{1,9},{9,1},{2,10},{10,2},{3,11},{11,3},{4,12},{12,4},... | collective-permute-start | bytes 1572872 | tf_op jit(solution)/shard_map/ppermute | solution.py:14
  128.7 30.9 %all-to-all-start.4 = ((bf16[32,16,1792]{2,1,0:T(8,128)(2,1)}), bf16[32,16,1792]{2,1,0:T(8,128)(2,1)S(1)}, u32[]{:S(2)}, u32[]{:S(2)}) async-start(bf16[32,16,1792]{2,1,0:T(8,128)(2,1)} %bitcast.111), calls=%async_computation.4 | async-start | bytes 3670016 | tf_op jit(solution)/shard_map/all_to_all | solution.py:57
  137.3 3.8 %collective-permute-start.4 = (f32[2,512,128]{2,1,0:T(8,128)S(1)}, f32[2,512,128]{2,1,0:T(8,128)S(1)}, u32[]{:S(2)}, u32[]{:S(2)}) collective-permute-start(f32[2,512,128]{2,1,0:T(8,128)S(1)} %fusion.9), channel_id=1, source_target_pairs={{0,8},{8,0},{1,9},{9,1},{2,10},{10,2},{3,11},{11,3},{4,12},{12,4},... | collective-permute-start | bytes 1572872 | tf_op jit(solution)/shard_map/ppermute | solution.py:14
  159.6 1.2 copy-start
  160.8 30.9 %all-to-all-start.5 = ((bf16[32,16,1792]{2,1,0:T(8,128)(2,1)}), bf16[32,16,1792]{2,1,0:T(8,128)(2,1)S(1)}, u32[]{:S(2)}, u32[]{:S(2)}) async-start(bf16[32,16,1792]{2,1,0:T(8,128)(2,1)} %bitcast.110), calls=%async_computation.5 | async-start | bytes 3670016 | tf_op jit(solution)/shard_map/all_to_all | solution.py:57
  167.4 2.4 copy-start.1
  179.3 31.3 %collective-permute-start.5 = (bf16[2,128,448]{1,2,0:T(8,128)(2,1)}, bf16[2,128,448]{1,2,0:T(8,128)(2,1)}, u32[]{:S(2)}, u32[]{:S(2)}) collective-permute-start(bf16[2,128,448]{1,2,0:T(8,128)(2,1)} %get-tuple-element.40), channel_id=1, source_target_pairs={{0,1},{1,0},{2,3},{3,2},{4,5},{5,4},{6,7},{7,6},{8,9},{9,8},{10,11... | collective-permute-start | bytes 688136 | tf_op jit(solution)/shard_map/ppermute | solution.py:93
  181.3 31.6 %collective-permute-start.6 = (bf16[2,128,448]{1,2,0:T(8,128)(2,1)S(1)}, bf16[2,128,448]{1,2,0:T(8,128)(2,1)}, u32[]{:S(2)}, u32[]{:S(2)}) collective-permute-start(bf16[2,128,448]{1,2,0:T(8,128)(2,1)S(1)} %get-tuple-element.42), channel_id=1, source_target_pairs={{0,2},{1,3},{2,0},{3,1},{4,6},{5,7},{6,4},{7,5},{8,10},{9,11},{10,... | collective-permute-start | bytes 688136 | tf_op jit(solution)/shard_map/ppermute | solution.py:93
  188.9 24.0 %collective-permute-start.7 = (bf16[2,128,448]{1,2,0:T(8,128)(2,1)S(1)}, bf16[2,128,448]{1,2,0:T(8,128)(2,1)}, u32[]{:S(2)}, u32[]{:S(2)}) collective-permute-start(bf16[2,128,448]{1,2,0:T(8,128)(2,1)S(1)} %get-tuple-element.41), channel_id=1, source_target_pairs={{0,3},{1,2},{2,1},{3,0},{4,7},{5,6},{6,5},{7,4},{8,11},{9,10},{10,... | collective-permute-start | bytes 688136 | tf_op jit(solution)/shard_map/ppermute | solution.py:93
  196.4 63.4 %all-to-all-start.6 = ((bf16[16,336,128]{2,1,0:T(8,128)(2,1)}), bf16[16,336,128]{2,1,0:T(8,128)(2,1)S(1)}, u32[]{:S(2)}, u32[]{:S(2)}) async-start(bf16[16,336,128]{2,1,0:T(8,128)(2,1)} %select_select_fusion), calls=%async_computation.6 | async-start | bytes 2752512 | tf_op jit(solution)/shard_map/all_to_all | solution.py:154
  202.2 22.0 %collective-permute-start.10 = (bf16[2,128,448]{1,2,0:T(8,128)(2,1)S(1)}, bf16[2,128,448]{1,2,0:T(8,128)(2,1)S(1)}, u32[]{:S(2)}, u32[]{:S(2)}) collective-permute-start(bf16[2,128,448]{1,2,0:T(8,128)(2,1)S(1)} %get-tuple-element.46), channel_id=1, source_target_pairs={{0,2},{1,3},{2,0},{3,1},{4,6},{5,7},{6,4},{7,5},{8,10},{9,11},{10,... | collective-permute-start | bytes 688136 | tf_op jit(solution)/shard_map/ppermute | solution.py:93
  207.6 16.6 %collective-permute-start.11 = (bf16[2,128,448]{1,2,0:T(8,128)(2,1)S(1)}, bf16[2,128,448]{1,2,0:T(8,128)(2,1)S(1)}, u32[]{:S(2)}, u32[]{:S(2)}) collective-permute-start(bf16[2,128,448]{1,2,0:T(8,128)(2,1)S(1)} %get-tuple-element.45), channel_id=1, source_target_pairs={{0,3},{1,2},{2,1},{3,0},{4,7},{5,6},{6,5},{7,4},{8,11},{9,10},{10,... | collective-permute-start | bytes 688136 | tf_op jit(solution)/shard_map/ppermute | solution.py:93
  210.7 20.2 %collective-permute-start.9 = (bf16[2,128,448]{1,2,0:T(8,128)(2,1)S(1)}, bf16[2,128,448]{1,2,0:T(8,128)(2,1)S(1)}, u32[]{:S(2)}, u32[]{:S(2)}) collective-permute-start(bf16[2,128,448]{1,2,0:T(8,128)(2,1)S(1)} %get-tuple-element.47), channel_id=1, source_target_pairs={{0,1},{1,0},{2,3},{3,2},{4,5},{5,4},{6,7},{7,6},{8,9},{9,8},{10,11... | collective-permute-start | bytes 688136 | tf_op jit(solution)/shard_map/ppermute | solution.py:93
  214.2 26.0 %collective-permute-start.8 = (bf16[128,448]{0,1:T(8,128)(2,1)S(1)}, bf16[128,448]{0,1:T(8,128)(2,1)S(1)}, u32[]{:S(2)}, u32[]{:S(2)}) collective-permute-start(bf16[128,448]{0,1:T(8,128)(2,1)S(1)} %dynamic-slice_bitcast_fusion.10), channel_id=1, source_target_pairs={{0,4},{4,0},{1,5},{5,1},{2,6},{6,2},{3,7},{7,3},{8,12},{12,8},{9,1... | collective-permute-start | bytes 344072 | tf_op jit(solution)/shard_map/ppermute | solution.py:14
  231.1 12.4 %collective-permute-start.12 = (bf16[128,448]{0,1:T(8,128)(2,1)S(1)}, bf16[128,448]{0,1:T(8,128)(2,1)S(1)}, u32[]{:S(2)}, u32[]{:S(2)}) collective-permute-start(bf16[128,448]{0,1:T(8,128)(2,1)S(1)} %get-tuple-element.48), channel_id=1, source_target_pairs={{0,23},{1,22},{2,21},{3,20},{4,19},{5,18},{6,17},{7,16},{16,7},{17... | collective-permute-start | bytes 344072 | tf_op jit(solution)/shard_map/ppermute | solution.py:18
  236.8 22.2 %collective-permute-start.13 = (bf16[128,448]{0,1:T(8,128)(2,1)S(1)}, bf16[128,448]{0,1:T(8,128)(2,1)S(1)}, u32[]{:S(2)}, u32[]{:S(2)}) collective-permute-start(bf16[128,448]{0,1:T(8,128)(2,1)S(1)} %get-tuple-element.49), channel_id=1, source_target_pairs={{0,19},{1,18},{2,17},{3,16},{4,23},{5,22},{6,21},{7,20},{16,3},{17... | collective-permute-start | bytes 344072 | tf_op jit(solution)/shard_map/ppermute | solution.py:162
